TPU v7x, 256 devices: a whole 4x4x8 slice. The times are simulated.
256 devices in a mesh: inp: 16 (over z, core), out: 16 (over x, y).
Axes of the slice: x: 4, y: 4, z: 8, core: 2. Of those that a mesh axis runs over, the one named last changes fastest.
Arguments:
- phases: bfloat16 [1024, 32768], P(None, 'inp'), may hold values from -3.140625 to 3.140625
- transfer_re: bfloat16 [32768, 4096], P('inp', 'out'), may hold values from -16 to 16
- transfer_im: bfloat16 [32768, 4096], P('inp', 'out'), may hold values from -16 to 16
- measured: float32 [1024, 4096], P(None, 'out'), may hold values from 0.1 to 4
Outputs:
- grad_re: float32 [32768, 4096], P('inp', 'out')
- grad_im: float32 [32768, 4096], P('inp', 'out')
All inputs are finite; a program needn't handle non-finite values.
Results may differ from a plain program's by a relative error of at most 0.0049.
Values may be sent and summed in bfloat16 or wider, within the bound.
A program may use at most 64 MiB of HBM per device.

v0:
```python
import jax
import jax.numpy as jnp
from jax import lax
from jax.sharding import PartitionSpec as P

P_SIZE = 1024


def transpose_product(left, right):
    return lax.dot_general(
        left, right, (((0,), (0,)), ((), ())), preferred_element_type=jnp.float32
    )


def body(phases, transfer_re, transfer_im, measured):
    angle = phases.astype(jnp.float32)
    probe_re = jnp.cos(angle).astype(jnp.bfloat16)
    probe_im = jnp.sin(angle).astype(jnp.bfloat16)
    norm = 1.0 / jnp.sqrt(jnp.float32(P_SIZE))
    part_re = jnp.dot(probe_re, transfer_re, preferred_element_type=jnp.float32) - jnp.dot(
        probe_im, transfer_im, preferred_element_type=jnp.float32
    )
    part_im = jnp.dot(probe_re, transfer_im, preferred_element_type=jnp.float32) + jnp.dot(
        probe_im, transfer_re, preferred_element_type=jnp.float32
    )
    field_re, field_im = lax.psum((part_re, part_im), "inp")
    power = field_re * field_re + field_im * field_im
    total_power, total_light = lax.psum((jnp.sum(power, axis=1), jnp.sum(measured, axis=1)), "out")
    scale = total_light / (total_power + 1e-05)
    factor = scale[:, None] * (scale[:, None] * power - measured)
    weight_re = (factor * field_re).astype(jnp.bfloat16)
    weight_im = (factor * field_im).astype(jnp.bfloat16)
    grad_re = (
        transpose_product(probe_re, weight_re) + transpose_product(probe_im, weight_im)
    ) * norm
    grad_im = (
        transpose_product(probe_re, weight_im) - transpose_product(probe_im, weight_re)
    ) * norm
    return (grad_re, grad_im)


def solution(mesh):
    in_specs = (P(None, "inp"), P("inp", "out"), P("inp", "out"), P(None, "out"))
    out_specs = (P("inp", "out"), P("inp", "out"))
    return jax.shard_map(body, mesh=mesh, in_specs=in_specs, out_specs=out_specs, check_vma=False)
```

profile of v0, /device:TPU:1, one launch (start us, length us, event | category | flops | bytes accessed | tf_op | source)
XLA Modules:
  0.0 420.5 jit_solution(2442946023220418237)
XLA Ops:
  7.2 0.0 copy-start
  7.2 0.0 all-reduce.4.cloned.1.call-start
  7.2 0.0 copy-start.1
  7.2 29.5 %fusion.6 = f32[1024,256]{1,0:T(8,128)S(1)} fusion(bf16[2048,256]{1,0:T(8,128)(2,1)} %param.5, bf16[1024,2048]{1,0:T(8,128)(2,1)} %param.4), kind=kOutput, calls=%fused_computation.6 | convolution fusion | flops 1077936128 | bytes 6291456 | tf_op jit(solution)/shard_map/dot_general | solution.py:23
  36.7 0.0 copy-done
  36.7 0.0 copy-done.1
  36.7 32.0 %fusion.8 = f32[1024,256]{1,0:T(8,128)S(1)} fusion(bf16[2048,256]{1,0:T(8,128)(2,1)S(1)} %copy-done, bf16[1024,2048]{1,0:T(8,128)(2,1)S(1)} %copy-done.1), kind=kOutput, calls=%fused_computation.7 | convolution fusion | flops 1077936128 | bytes 6291456 | tf_op jit(solution)/shard_map/dot_general | solution.py:20
  68.7 0.0 copy-start.5
  68.7 32.5 %fusion.39 = f32[1024,256]{1,0:T(8,128)} fusion(f32[1024,256]{1,0:T(8,128)S(1)} %fusion.6, bf16[2048,256]{1,0:T(8,128)(2,1)S(1)} %copy-done, bf16[1024,2048]{1,0:T(8,128)(2,1)S(1)} %copy-done.1), kind=kOutput, calls=%fused_computation.19 | convolution fusion | flops 1078198272 | bytes 7340032 | tf_op jit(solution)/shard_map/dot_general | solution.py:23
  101.2 32.5 %fusion.36 = f32[1024,256]{1,0:T(8,128)} fusion(f32[1024,256]{1,0:T(8,128)S(1)} %fusion.8, bf16[2048,256]{1,0:T(8,128)(2,1)S(1)} %copy-done.5, bf16[1024,2048]{1,0:T(8,128)(2,1)S(1)} %copy-done.1), kind=kOutput, calls=%fused_computation.18 | convolution fusion | flops 1078198272 | bytes 7340032 | tf_op jit(solution)/shard_map/dot_general | solution.py:20
  133.7 0.0 all-reduce.4.cloned.1.call-update
  133.7 0.2 reduce_sum.18
  134.0 118.6 %all-reduce.4.cloned.1.call-done = (f32[1024,256]{1,0:T(8,128)}, f32[1024,256]{1,0:T(8,128)}) async-done(((f32[1024,256]{1,0:T(8,128)}, f32[1024,256]{1,0:T(8,128)}), (f32[1024,256]{1,0:T(8,128)}, f32[1024,256]{1,0:T(8,128)})) %all-reduce.4.cloned.1.call-update) | async-done | bytes 2097168 | tf_op jit(solution)/shard_map/psum | solution.py:26
  252.5 1.8 fusion.42
  254.3 33.8 %all-reduce = (f32[1024]{0:T(1024)S(1)}, f32[1024]{0:T(1024)S(1)}) all-reduce(f32[1024]{0:T(1024)S(1)} %reduce_sum.18, f32[1024]{0:T(1024)S(1)} %fusion.42), channel_id=1, replica_groups=mesh['inp'=16,'out'=16] {'out'}, use_global_device_ids=true, to_apply=%region_1.0 | all-reduce | flops 2048 | bytes 16384 | tf_op jit(solution)/shard_map/psum | solution.py:28
  288.1 0.0 copy-start.2
  288.1 2.0 multiply_convert_fusion.1
  290.1 0.7 copy-done.2
  290.9 28.7 %fusion.2 = f32[256,2048]{1,0:T(8,128)S(1)} fusion(bf16[1024,256]{1,0:T(8,128)(2,1)S(1)} %get-tuple-element.8, bf16[1024,2048]{1,0:T(8,128)(2,1)S(1)} %copy-done.2), kind=kOutput, calls=%fused_computation.4 | convolution fusion | flops 1077936128 | bytes 6815744 | tf_op jit(solution)/shard_map/dot_general | solution.py:10
  319.6 28.7 %fusion.4 = f32[256,2048]{1,0:T(8,128)S(1)} fusion(bf16[1024,256]{1,0:T(8,128)(2,1)S(1)} %get-tuple-element.9, bf16[1024,2048]{1,0:T(8,128)(2,1)S(1)} %copy-done.2), kind=kOutput, calls=%fused_computation.5 | convolution fusion | flops 1077936128 | bytes 6815744 | tf_op jit(solution)/shard_map/dot_general | solution.py:10
  348.3 29.2 %fusion.27 = f32[2048,256]{0,1:T(8,128)} fusion(f32[256,2048]{1,0:T(8,128)S(1)} %fusion.2, bf16[1024,256]{1,0:T(8,128)(2,1)S(1)} %get-tuple-element.9, bf16[1024,2048]{1,0:T(8,128)(2,1)S(1)} %copy-done.2), kind=kOutput, calls=%fused_computation.15 | convolution fusion | flops 1078984704 | bytes 8912896 | tf_op jit(solution)/shard_map/dot_general | solution.py:10
  377.5 2.9 copy.7
  380.3 30.4 %fusion.33 = f32[2048,256]{0,1:T(8,128)} fusion(f32[256,2048]{1,0:T(8,128)S(1)} %fusion.4, bf16[1024,256]{1,0:T(8,128)(2,1)} %copy-done.3, bf16[1024,2048]{1,0:T(8,128)(2,1)} %param.4), kind=kOutput, calls=%fused_computation.17 | convolution fusion | flops 1078984704 | bytes 8912896 | tf_op jit(solution)/shard_map/dot_general | solution.py:10
  410.8 2.9 copy.6
  (6 shorter events, 0.0 us)
Async XLA Ops:
  7.2 29.6 %copy-start = (bf16[2048,256]{1,0:T(8,128)(2,1)S(1)}, bf16[2048,256]{1,0:T(8,128)(2,1)}, u32[]{:S(2)}) copy-start(bf16[2048,256]{1,0:T(8,128)(2,1)} %param.6) | copy-start | bytes 3145732
  7.2 245.3 %all-reduce.4.cloned.1.call-start = ((), (), s32[]{:S(2)}) async-start(), calls=%async_computation | async-start | bytes 4194304 | tf_op jit(solution)/shard_map/psum | solution.py:26
  7.2 29.5 %copy-start.1 = (bf16[1024,2048]{1,0:T(8,128)(2,1)S(1)}, bf16[1024,2048]{1,0:T(8,128)(2,1)}, u32[]{:S(2)}) copy-start(bf16[1024,2048]{1,0:T(8,128)(2,1)} %param.4) | copy-start | bytes 12582916
  68.7 32.5 %copy-start.5 = (bf16[2048,256]{1,0:T(8,128)(2,1)S(1)}, bf16[2048,256]{1,0:T(8,128)(2,1)}, u32[]{:S(2)}) copy-start(bf16[2048,256]{1,0:T(8,128)(2,1)} %param.5) | copy-start | bytes 3145732
  101.2 32.5 %copy-start.4 = (f32[1024,256]{1,0:T(8,128)S(1)}, f32[1024,256]{1,0:T(8,128)}, u32[]{:S(2)}) copy-start(f32[1024,256]{1,0:T(8,128)} %param.7) | copy-start | bytes 3145732
  288.1 2.8 copy-start.2
  290.1 58.1 %copy-start.3 = (bf16[1024,256]{1,0:T(8,128)(2,1)}, bf16[1024,256]{1,0:T(8,128)(2,1)S(1)}, u32[]{:S(2)}) copy-start(bf16[1024,256]{1,0:T(8,128)(2,1)S(1)} %get-tuple-element.8) | copy-start | bytes 1572868
Sparse Core Ops, SparseCore 0:
  133.8 118.6 all-reduce.3
where the time goes:
time: 426 us; the launch traced here: 420 us
  matrix products  243 us (57%)
  waiting for transfers between devices  119 us (28%)
  blocking collectives  33.8 us (8%)
  between operations  14.2 us (3%)
  local copies, waits for them, and re-layouts  6.54 us (2%)
    psum x1, waiting for transfers between devices, body(): field_re, field_im = lax.psum((part_re, part_im), 'inp')  119 us
    dot_general x4, matrix products, transpose_product(): lax.dot_general(left, right, (((0,), (0,)), ((), ())), preferred_element_...  117 us
    psum x1, blocking collectives, body(): lax.psum((jnp.sum(power, axis=1), jnp.sum(measured, axis=1)), 'out')  33.8 us
    dot_general x1, matrix products, body(): jnp.dot(probe_re, transfer_im, preferred_element_type=jnp.float32)  32.5 us
    dot_general x1, matrix products, body(): jnp.dot(probe_re, transfer_re, preferred_element_type=jnp.float32)  32.5 us
    dot_general x1, matrix products, body(): jnp.dot(probe_im, transfer_im, preferred_element_type=jnp.float32)  32 us
    dot_general x1, matrix products, body(): jnp.dot(probe_im, transfer_re, preferred_element_type=jnp.float32)  29.5 us
  transfers between devices with their start and end apart: 1, of which 1 were waited for; matrix products, arithmetic and copies ran while one was open for 0% of the time, Pallas kernels for 0%

commit v1 on v0

v1 whole, which is shorter than its diff:
```python
import functools

import jax
import jax.numpy as jnp
from jax import lax
from jax.experimental import pallas as pl
from jax.experimental.pallas import tpu as pltpu
from jax.sharding import PartitionSpec as P

P_SIZE = 1024
MESH = pl.DeviceIdType.MESH
F32 = jnp.float32
BF16 = jnp.bfloat16
SIN = (7.07104388e-01, -2.94595328e-02, 3.67091170e-04, -2.02891555e-06)
COS = (1.41421350e00, -1.76776361e-01, 3.68257540e-03, -3.06126501e-05, 1.27908569e-07)


def cos_sin(x):
    u = x * x
    s = x * (SIN[0] + u * (SIN[1] + u * (SIN[2] + u * SIN[3])))
    c = COS[0] + u * (COS[1] + u * (COS[2] + u * (COS[3] + u * COS[4])))
    return 1.0 - s * s, s * c


def twice(w, n):
    return jnp.concatenate([w, jnp.concatenate([w[:, n:], -w[:, :n]], axis=1)], axis=0)


def front(
    zs, outs, ph_hbm, tr_hbm, ti_hbm, me_hbm, acc_hbm, pt_hbm, w_hbm,
    ph, rhs, meas, pt, acc, part, give, sib, ring, send, field, pw, pws, w,
    in_sem, t_sem, o_sem, sib_s, sib_r, ring_s, ring_r, pw_s, pw_r,
    agl_s, agl_r, ags_s, ags_r, agb_s, agb_r,
):
    chunk, half, n = ph.shape[1], ph.shape[1] // 2, meas.shape[1]
    depth, slab = ph.shape[2], min(256, ph.shape[2])
    sub = half // 2
    me = lax.axis_index("inp")
    peer = lax.axis_index("out")
    z, core = me // 2, me % 2
    step = 1 - 2 * core
    ahead = lax.rem(z + step + zs, zs) * 2 + core
    behind = lax.rem(z - step + zs, zs) * 2 + core
    other = z * 2 + 1 - core
    mine = pl.multiple_of(core * half, half)
    theirs = pl.multiple_of((1 - core) * half, half)

    def chunk_of(i):
        off = jnp.where(i % 2 == 1, 4 - (i + 1) // 2, i // 2 - 4)
        return lax.rem(z + off + zs, zs)

    def load_phase(i):
        rows = pl.ds(pl.multiple_of(chunk_of(i) * chunk, chunk), chunk)
        return pltpu.make_async_copy(ph_hbm.at[rows], ph.at[i], in_sem.at[i])

    loads = [
        pltpu.make_async_copy(tr_hbm, rhs.at[0, :, pl.ds(0, n)], t_sem.at[0]),
        pltpu.make_async_copy(ti_hbm, rhs.at[0, :, pl.ds(n, n)], t_sem.at[1]),
        pltpu.make_async_copy(tr_hbm, rhs.at[1, :, pl.ds(n, n)], t_sem.at[2]),
    ]
    load_phase(0).start()
    for copy in loads:
        copy.start()
    for i in range(1, zs):
        load_phase(i).start()
    own_rows = pl.ds(pl.multiple_of(z * chunk + core * half, half), half)
    load_meas = pltpu.make_async_copy(me_hbm.at[own_rows], meas, t_sem.at[3])
    load_meas.start()

    barrier = pltpu.get_barrier_semaphore()
    for target in (other, ahead, behind):
        pl.semaphore_signal(barrier, inc=1, device_id={"inp": target}, device_id_type=MESH)
    for j in range(1, outs):
        pl.semaphore_signal(
            barrier, inc=1, device_id={"out": lax.rem(peer + j, outs)}, device_id_type=MESH
        )

    for copy in loads:
        copy.wait()
    rhs[1, :, 0:n] = -rhs[0, :, n:]

    def to_sibling(i):
        return pltpu.make_async_remote_copy(
            src_ref=give.at[i], dst_ref=sib.at[i], send_sem=sib_s.at[i], recv_sem=sib_r.at[i],
            device_id={"inp": other}, device_id_type=MESH,
        )

    def round_ring(e, h):
        target = jnp.where(e % 2 == 0, ahead, behind)
        rows = pl.ds(h * sub, sub)
        return pltpu.make_async_remote_copy(
            src_ref=send.at[e, rows], dst_ref=ring.at[e, rows],
            send_sem=ring_s.at[e, h], recv_sem=ring_r.at[e, h],
            device_id={"inp": target}, device_id_type=MESH,
        )

    def forward(i):
        load_phase(i).wait()
        total = None
        for j in range(depth // slab):
            cols = slice(j * slab, (j + 1) * slab)
            re, im = cos_sin(ph[i, :, cols].astype(F32))
            re, im = re.astype(BF16), im.astype(BF16)
            pt[i, cols, 0:chunk] = re.T
            pt[i, cols, chunk:] = im.T
            left = jnp.concatenate([re, im], axis=1)
            right = jnp.concatenate([rhs[0, cols, :], rhs[1, cols, :]], axis=0)
            term = jnp.dot(left, right, preferred_element_type=F32)
            total = term if total is None else total + term
        field[...] = total
        part[i] = field[pl.ds(mine, half), :]
        give[i] = field[pl.ds(theirs, half), :]

    def event(e):
        swap = jnp.where((e >= 1) & (e <= 6), jnp.where(e % 2 == 1, 1, -1), 0)
        i = e + swap * (1 - core)
        to_sibling(i).wait_recv()
        for h in range(2):
            rows = slice(h * sub, (h + 1) * sub)
            value = part[i, rows, :] + sib[i, rows, :]

            @pl.when(e < 2)
            def _():
                send[e, rows, :] = value

            @pl.when(e >= 2)
            def _():
                round_ring(e - 2, h).wait_recv()
                send[e, rows, :] = value + ring[e - 2, rows, :]

            round_ring(e, h).start()

    def body(i, _):
        forward(i)

        @pl.when(i == 0)
        def _():
            pl.semaphore_wait(barrier, 3 + outs - 1)

        to_sibling(i).start()

        @pl.when(i >= 1)
        def _():
            event(i - 1)

        return 0

    lax.fori_loop(0, zs, body, 0)

    load_meas.wait()
    light = meas[...]
    to_sibling(zs - 1).wait_recv()
    total = part[zs - 1] + sib[zs - 1]
    for h in range(2):
        round_ring(zs - 3, h).wait_recv()
    total = total + ring[zs - 3]
    for h in range(2):
        round_ring(zs - 2, h).wait_recv()
    total = total + ring[zs - 2]
    f_re, f_im = total[:, :n], total[:, n:]
    power = f_re * f_re + f_im * f_im

    def lane_sum(v):
        folded = v[:, 0:128]
        for k in range(1, n // 128):
            folded = folded + v[:, k * 128 : (k + 1) * 128]
        return jnp.sum(folded.T, axis=0, keepdims=True)

    pws[...] = jnp.concatenate(
        [lane_sum(power), lane_sum(light), jnp.zeros((6, half), F32)], axis=0
    )

    def to_peer(j):
        return pltpu.make_async_remote_copy(
            src_ref=pws, dst_ref=pw.at[j], send_sem=pw_s.at[j], recv_sem=pw_r.at[j],
            device_id={"out": lax.rem(peer + j, outs)}, device_id_type=MESH,
        )

    for j in range(1, outs):
        to_peer(j).start()
    sums = pws[...]
    for j in range(1, outs):
        to_peer(j).wait_recv()
        sums = sums + pw[j]
    scale = sums[1:2, :] / (sums[0:1, :] + 1e-05)
    scale = jnp.broadcast_to(scale, (128, half)).T
    scale = jnp.concatenate([scale] * (n // 128), axis=1)
    factor = scale * (scale * power - light)
    own = pl.ds(mine, half)
    w[zs - 1, own, 0:n] = (factor * f_re).astype(BF16)
    w[zs - 1, own, n:] = (factor * f_im).astype(BF16)

    def long_slot(t):
        return zs - 1 if t == 0 else 8 - 2 * t - (core if t < 4 else 0)

    def short_slot(t):
        return zs - 1 if t == 0 else 7 - 2 * t + core

    def pass_on(slot_of, sems, target, t, h):
        rows = pl.ds(pl.multiple_of(mine + h * sub, sub), sub)
        slot = slot_of(t)
        there = slot_of(t + 1)
        return pltpu.make_async_remote_copy(
            src_ref=w.at[slot, rows], dst_ref=w.at[there, rows],
            send_sem=sems[0].at[t, h], recv_sem=sems[1].at[t, h],
            device_id={"inp": target}, device_id_type=MESH,
        )

    def go_long(t, h):
        return pass_on(long_slot, (agl_s, agl_r), ahead, t, h)

    def go_short(t, h):
        return pass_on(short_slot, (ags_s, ags_r), behind, t, h)

    def share(slot, h, rows0):
        rows = pl.ds(pl.multiple_of(rows0 + h * sub, sub), sub)
        return pltpu.make_async_remote_copy(
            src_ref=w.at[slot, rows], dst_ref=w.at[slot, rows],
            send_sem=agb_s.at[slot, h], recv_sem=agb_r.at[slot, h],
            device_id={"inp": other}, device_id_type=MESH,
        )

    for h in range(2):
        go_long(0, h).start()
        go_short(0, h).start()
    for h in range(2):
        share(zs - 1, h, mine).start()

    block = min(256, depth)

    def backward(slots, first):
        def rows_of(b, _):
            rows = pl.ds(pl.multiple_of(b * block, block), block)
            value = None
            for s in slots:
                term = jnp.dot(pt[s, rows, :], twice(w[s], n), preferred_element_type=F32)
                value = term if value is None else value + term
            if not first:
                value = value + acc[rows, :]
            acc[rows, :] = value
            return 0

        lax.fori_loop(0, depth // block, rows_of, 0)

    for t in range(1, 5):
        for h in range(2):
            go_long(t - 1, h).wait_recv()
            if t < 4:
                go_long(t, h).start()
            share(long_slot(t), h, mine).start()
            if t < 4:
                go_short(t - 1, h).wait_recv()
                if t < 3:
                    go_short(t, h).start()
                share(short_slot(t), h, mine).start()
        slots = (zs - 1,) if t == 1 else (9 - 2 * t, 10 - 2 * t)
        for s in slots:
            for h in range(2):
                share(s, h, theirs).wait_recv()
        backward(slots, t == 1)

    out_acc = pltpu.make_async_copy(acc, acc_hbm, o_sem.at[0])
    out_acc.start()
    out_pt = pltpu.make_async_copy(pt.at[0], pt_hbm, o_sem.at[1])
    out_pt.start()
    for h in range(2):
        share(0, h, theirs).wait_recv()
    out_w = pltpu.make_async_copy(w.at[0], w_hbm, o_sem.at[2])
    out_w.start()

    def drain(i, _):
        to_sibling(i).wait_send()
        for h in range(2):
            share(i, h, mine).wait_send()
        return 0

    lax.fori_loop(0, zs, drain, 0)

    def drain_ring(e, _):
        for h in range(2):
            round_ring(e, h).wait_send()
        return 0

    lax.fori_loop(0, zs - 1, drain_ring, 0)
    for j in range(1, outs):
        to_peer(j).wait_send()
    for h in range(2):
        for t in range(4):
            go_long(t, h).wait_send()
        for t in range(3):
            go_short(t, h).wait_send()
    out_acc.wait()
    out_pt.wait()
    out_w.wait()


def finish(acc, pt, w, re, im):
    n = re.shape[1]
    value = acc[...] + jnp.dot(pt[...], twice(w[...], n), preferred_element_type=F32)
    norm = 1.0 / float(P_SIZE) ** 0.5
    re[...] = value[:, :n] * norm
    im[...] = value[:, n:] * norm


def body(zs, outs, phases, transfer_re, transfer_im, measured):
    probes, depth = phases.shape
    n = transfer_re.shape[1]
    chunk = probes // zs
    half = chunk // 2
    DMA = pltpu.SemaphoreType.DMA
    anywhere = pl.BlockSpec(memory_space=pl.ANY)
    acc, pt, w = pl.pallas_call(
        functools.partial(front, zs, outs),
        out_shape=(
            jax.ShapeDtypeStruct((depth, 2 * n), F32),
            jax.ShapeDtypeStruct((depth, 2 * chunk), BF16),
            jax.ShapeDtypeStruct((chunk, 2 * n), BF16),
        ),
        in_specs=[anywhere] * 4,
        out_specs=(anywhere,) * 3,
        scratch_shapes=[
            pltpu.VMEM((zs, chunk, depth), BF16),
            pltpu.VMEM((2, depth, 2 * n), BF16),
            pltpu.VMEM((half, n), F32),
            pltpu.VMEM((zs, depth, 2 * chunk), BF16),
            pltpu.VMEM((depth, 2 * n), F32),
            pltpu.VMEM((zs, half, 2 * n), F32),
            pltpu.VMEM((zs, half, 2 * n), F32),
            pltpu.VMEM((zs, half, 2 * n), F32),
            pltpu.VMEM((zs - 1, half, 2 * n), F32),
            pltpu.VMEM((zs - 1, half, 2 * n), F32),
            pltpu.VMEM((chunk, 2 * n), F32),
            pltpu.VMEM((outs, 8, half), F32),
            pltpu.VMEM((8, half), F32),
            pltpu.VMEM((zs, chunk, 2 * n), BF16),
            DMA((zs,)), DMA((4,)), DMA((3,)),
            DMA((zs,)), DMA((zs,)),
            DMA((zs - 1, 2)), DMA((zs - 1, 2)),
            DMA((outs,)), DMA((outs,)),
            DMA((4, 2)), DMA((4, 2)), DMA((3, 2)), DMA((3, 2)),
            DMA((zs, 2)), DMA((zs, 2)),
        ],
        compiler_params=pltpu.CompilerParams(
            collective_id=0, has_side_effects=True, vmem_limit_bytes=50 * 1024 * 1024
        ),
    )(phases, transfer_re, transfer_im, measured)
    block = min(512, depth)
    return pl.pallas_call(
        finish,
        grid=(depth // block,),
        out_shape=(jax.ShapeDtypeStruct((depth, n), F32),) * 2,
        in_specs=[
            pl.BlockSpec((block, 2 * n), lambda b: (b, 0)),
            pl.BlockSpec((block, 2 * chunk), lambda b: (b, 0)),
            pl.BlockSpec((chunk, 2 * n), lambda b: (0, 0)),
        ],
        out_specs=(pl.BlockSpec((block, n), lambda b: (b, 0)),) * 2,
    )(acc, pt, w)


def solution(mesh):
    in_specs = (P(None, "inp"), P("inp", "out"), P("inp", "out"), P(None, "out"))
    out_specs = (P("inp", "out"), P("inp", "out"))
    fn = functools.partial(body, mesh.shape["inp"] // 2, mesh.shape["out"])
    return jax.shard_map(fn, mesh=mesh, in_specs=in_specs, out_specs=out_specs, check_vma=False)
```

time: 426 us -> 61.5 us (0.14); the launches traced: 420 us -> 60.8 us
  matrix products: 243 us -> 0 us
  waiting for transfers between devices: 119 us -> 0 us
  Pallas kernels: 0 us -> 56.1 us
  blocking collectives: 33.8 us -> 0 us
  between operations: 14.2 us -> 0.66 us
    dot_general x8 -> x0, matrix products: 243 us -> none  [the longest x4 117 us: transpose_product(): lax.dot_general(left, right, (((0,), (0,)), ((), ())), preferred_element_...]
    psum x1 -> x0, waiting for transfers between devices: 119 us -> none  [body(): field_re, field_im = lax.psum((part_re, part_im), 'inp')]
    pallas_call x0 -> x2, Pallas kernels: none -> 56.1 us  [the longest x1 50.8 us: body(): pl.pallas_call(functools.partial(front, zs, outs), out_shape=(jax.ShapeDt...]
    psum x1 -> x0, blocking collectives: 33.8 us -> none  [body(): lax.psum((jnp.sum(power, axis=1), jnp.sum(measured, axis=1)), 'out')]
  transfers between devices with their start and end apart: 1 -> 0, of which waited for: 1 -> 0; matrix products, arithmetic and copies ran while one was open for 0% -> 0% of each run, Pallas kernels for 0% -> 0%
where the time goes in v1:
time: 61.5 us; the launch traced here: 60.8 us
  Pallas kernels  56.1 us (91%)
  local copies, waits for them, and re-layouts  4.06 us (7%)
  between operations  0.66 us (1%)
    pallas_call x1, Pallas kernels, body(): pl.pallas_call(functools.partial(front, zs, outs), out_shape=(jax.ShapeDt...  50.8 us
    pallas_call x1, Pallas kernels, body(): pl.pallas_call(finish, grid=(depth // block,), out_shape=(jax.ShapeDtypeS...  5.33 us
    unnamed x8, local copies, waits for them, and re-layouts  4.06 us

profile of v1, /device:TPU:1, one launch (start us, length us, event | category | flops | bytes accessed | tf_op | source)
XLA Modules:
  0.0 60.8 jit_solution(12037425648630299794)
XLA Ops:
  0.6 0.0 copy-start
  0.6 1.2 %copy-done = bf16[2048,256]{1,0:T(8,128)(2,1)S(1)} copy-done((bf16[2048,256]{1,0:T(8,128)(2,1)S(1)}, bf16[2048,256]{1,0:T(8,128)(2,1)}, u32[]{:S(2)}) %copy-start) | copy-done | bytes 1048600
  1.9 0.0 copy-start.1
  1.9 1.2 %copy-done.1 = bf16[2048,256]{1,0:T(8,128)(2,1)S(1)} copy-done((bf16[2048,256]{1,0:T(8,128)(2,1)S(1)}, bf16[2048,256]{1,0:T(8,128)(2,1)}, u32[]{:S(2)}) %copy-start.1) | copy-done | bytes 1048600
  3.1 50.8 %shard_map.59 = (f32[2048,512]{1,0:T(8,128)}, bf16[2048,256]{1,0:T(8,128)(2,1)S(1)}, bf16[128,512]{1,0:T(8,128)(2,1)S(1)}) custom-call(bf16[1024,2048]{1,0:T(8,128)(2,1)} %ph_hbm.1, bf16[2048,256]{1,0:T(8,128)(2,1)S(1)} %copy-done, bf16[2048,256]{1,0:T(8,128)(2,1)S(1)} %copy-done.1, f32[1024,256]{1,0:T(8,128)} %me_hbm.1), custom_call_target="tpu_custom_call" | custom-call | tf_op jit(solution)/shard_map/pallas_call | solution.py:312
  53.8 0.0 copy-start.2
  53.9 1.0 %copy-done.2 = bf16[2048,256]{1,0:T(8,128)(2,1)} copy-done((bf16[2048,256]{1,0:T(8,128)(2,1)}, bf16[2048,256]{1,0:T(8,128)(2,1)S(1)}, u32[]{:S(2)}) %copy-start.2) | copy-done | bytes 1048600
  54.8 0.0 copy-start.3
  54.8 0.6 %copy-done.3 = bf16[128,512]{1,0:T(8,128)(2,1)} copy-done((bf16[128,512]{1,0:T(8,128)(2,1)}, bf16[128,512]{1,0:T(8,128)(2,1)S(1)}, u32[]{:S(2)}) %copy-start.3) | copy-done | bytes 131096
  55.5 5.3 %shard_map.60 = (f32[2048,256]{1,0:T(8,128)}, f32[2048,256]{1,0:T(8,128)}) custom-call(f32[2048,512]{1,0:T(8,128)} %get-tuple-element.5.acc, bf16[2048,256]{1,0:T(8,128)(2,1)} %copy-done.2, bf16[128,512]{1,0:T(8,128)(2,1)} %copy-done.3), custom_call_target="tpu_custom_call" | custom-call | tf_op jit(solution)/shard_map/pallas_call | solution.py:348
Async XLA Ops:
  0.6 1.2 %copy-start = (bf16[2048,256]{1,0:T(8,128)(2,1)S(1)}, bf16[2048,256]{1,0:T(8,128)(2,1)}, u32[]{:S(2)}) copy-start(bf16[2048,256]{1,0:T(8,128)(2,1)} %tr_hbm.1) | copy-start | bytes 3145732
  1.9 1.2 %copy-start.1 = (bf16[2048,256]{1,0:T(8,128)(2,1)S(1)}, bf16[2048,256]{1,0:T(8,128)(2,1)}, u32[]{:S(2)}) copy-start(bf16[2048,256]{1,0:T(8,128)(2,1)} %ti_hbm.1) | copy-start | bytes 3145732
  53.8 1.0 %copy-start.2 = (bf16[2048,256]{1,0:T(8,128)(2,1)}, bf16[2048,256]{1,0:T(8,128)(2,1)S(1)}, u32[]{:S(2)}) copy-start(bf16[2048,256]{1,0:T(8,128)(2,1)S(1)} %get-tuple-element.6.pt) | copy-start | bytes 3145732
  54.8 0.6 %copy-start.3 = (bf16[128,512]{1,0:T(8,128)(2,1)}, bf16[128,512]{1,0:T(8,128)(2,1)S(1)}, u32[]{:S(2)}) copy-start(bf16[128,512]{1,0:T(8,128)(2,1)S(1)} %get-tuple-element.7.w) | copy-start | bytes 393220

commit v2 on v1

--- a/solution.py
+++ b/solution.py
@@ -9,6 +9,9 @@
 
 P_SIZE = 1024
 MESH = pl.DeviceIdType.MESH
+TREE = ((0, 2), (0, -2), (0, 1), (0, -1), (2, 4), (2, 3), (-2, -3))
+LATE = 3
+PIECES = 4
 F32 = jnp.float32
 BF16 = jnp.bfloat16
 SIN = (7.07104388e-01, -2.94595328e-02, 3.67091170e-04, -2.02891555e-06)
@@ -27,10 +30,9 @@
 
 
 def front(
-    zs, outs, ph_hbm, tr_hbm, ti_hbm, me_hbm, acc_hbm, pt_hbm, w_hbm,
-    ph, rhs, meas, pt, acc, part, give, sib, ring, send, field, pw, pws, w,
-    in_sem, t_sem, o_sem, sib_s, sib_r, ring_s, ring_r, pw_s, pw_r,
-    agl_s, agl_r, ags_s, ags_r, agb_s, agb_r,
+    zs, outs, ph_hbm, tr_hbm, ti_hbm, me_hbm, acc, pt, w_late,
+    ph, rhs, meas, part, give, sib, ring, send, field, pw, pws, w,
+    in_sem, t_sem, sib_s, sib_r, ring_s, ring_r, pw_s, pw_r, ag_s, ag_r, agb_s, agb_r,
 ):
     chunk, half, n = ph.shape[1], ph.shape[1] // 2, meas.shape[1]
     depth, slab = ph.shape[2], min(256, ph.shape[2])
@@ -39,8 +41,11 @@
     peer = lax.axis_index("out")
     z, core = me // 2, me % 2
     step = 1 - 2 * core
-    ahead = lax.rem(z + step + zs, zs) * 2 + core
-    behind = lax.rem(z - step + zs, zs) * 2 + core
+
+    def at(d):
+        return lax.rem(z + step * d + zs, zs) * 2 + core
+
+    ahead, behind = at(1), at(-1)
     other = z * 2 + 1 - core
     mine = pl.multiple_of(core * half, half)
     theirs = pl.multiple_of((1 - core) * half, half)
@@ -68,7 +73,7 @@
     load_meas.start()
 
     barrier = pltpu.get_barrier_semaphore()
-    for target in (other, ahead, behind):
+    for target in (other, ahead, behind, at(2), at(-2)):
         pl.semaphore_signal(barrier, inc=1, device_id={"inp": target}, device_id_type=MESH)
     for j in range(1, outs):
         pl.semaphore_signal(
@@ -135,7 +140,7 @@
 
         @pl.when(i == 0)
         def _():
-            pl.semaphore_wait(barrier, 3 + outs - 1)
+            pl.semaphore_wait(barrier, 5 + outs - 1)
 
         to_sibling(i).start()
 
@@ -190,45 +195,43 @@
     w[zs - 1, own, 0:n] = (factor * f_re).astype(BF16)
     w[zs - 1, own, n:] = (factor * f_im).astype(BF16)
 
-    def long_slot(t):
-        return zs - 1 if t == 0 else 8 - 2 * t - (core if t < 4 else 0)
-
-    def short_slot(t):
-        return zs - 1 if t == 0 else 7 - 2 * t + core
-
-    def pass_on(slot_of, sems, target, t, h):
-        rows = pl.ds(pl.multiple_of(mine + h * sub, sub), sub)
-        slot = slot_of(t)
-        there = slot_of(t + 1)
-        return pltpu.make_async_remote_copy(
-            src_ref=w.at[slot, rows], dst_ref=w.at[there, rows],
-            send_sem=sems[0].at[t, h], recv_sem=sems[1].at[t, h],
-            device_id={"inp": target}, device_id_type=MESH,
-        )
-
-    def go_long(t, h):
-        return pass_on(long_slot, (agl_s, agl_r), ahead, t, h)
-
-    def go_short(t, h):
-        return pass_on(short_slot, (ags_s, ags_r), behind, t, h)
-
-    def share(slot, h, rows0):
-        rows = pl.ds(pl.multiple_of(rows0 + h * sub, sub), sub)
+    def slot_of(d):
+        if d == 0:
+            return zs - 1
+        if d == 4:
+            return 0
+        return 8 - 2 * d - core if d > 0 else 7 + 2 * d + core
+
+    def pass_on(k):
+        d, there = TREE[k]
+        rows = pl.ds(mine, half)
+        return pltpu.make_async_remote_copy(
+            src_ref=w.at[slot_of(d), rows], dst_ref=w.at[slot_of(there), rows],
+            send_sem=ag_s.at[k], recv_sem=ag_r.at[k],
+            device_id={"inp": at(there - d)}, device_id_type=MESH,
+        )
+
+    def share(slot, rows0):
+        rows = pl.ds(rows0, half)
         return pltpu.make_async_remote_copy(
             src_ref=w.at[slot, rows], dst_ref=w.at[slot, rows],
-            send_sem=agb_s.at[slot, h], recv_sem=agb_r.at[slot, h],
+            send_sem=agb_s.at[slot], recv_sem=agb_r.at[slot],
             device_id={"inp": other}, device_id_type=MESH,
         )
 
-    for h in range(2):
-        go_long(0, h).start()
-        go_short(0, h).start()
-    for h in range(2):
-        share(zs - 1, h, mine).start()
-
-    block = min(256, depth)
+    def arrive(k):
+        pass_on(k).wait_recv()
+        for later in range(len(TREE)):
+            if TREE[later][0] == TREE[k][1]:
+                pass_on(later).start()
+        share(slot_of(TREE[k][1]), mine).start()
+
+    block = min(512, depth)
 
     def backward(slots, first):
+        for s in slots:
+            share(s, theirs).wait_recv()
+
         def rows_of(b, _):
             rows = pl.ds(pl.multiple_of(b * block, block), block)
             value = None
@@ -242,36 +245,22 @@
 
         lax.fori_loop(0, depth // block, rows_of, 0)
 
-    for t in range(1, 5):
-        for h in range(2):
-            go_long(t - 1, h).wait_recv()
-            if t < 4:
-                go_long(t, h).start()
-            share(long_slot(t), h, mine).start()
-            if t < 4:
-                go_short(t - 1, h).wait_recv()
-                if t < 3:
-                    go_short(t, h).start()
-                share(short_slot(t), h, mine).start()
-        slots = (zs - 1,) if t == 1 else (9 - 2 * t, 10 - 2 * t)
-        for s in slots:
-            for h in range(2):
-                share(s, h, theirs).wait_recv()
-        backward(slots, t == 1)
-
-    out_acc = pltpu.make_async_copy(acc, acc_hbm, o_sem.at[0])
-    out_acc.start()
-    out_pt = pltpu.make_async_copy(pt.at[0], pt_hbm, o_sem.at[1])
-    out_pt.start()
-    for h in range(2):
-        share(0, h, theirs).wait_recv()
-    out_w = pltpu.make_async_copy(w.at[0], w_hbm, o_sem.at[2])
-    out_w.start()
+    for k in range(4):
+        pass_on(k).start()
+    share(zs - 1, mine).start()
+    backward((zs - 1,), True)
+    for k in (0, 1, 2, 3):
+        arrive(k)
+    backward((3, 4, 5, 6), False)
+    for k in (6, 5, 4):
+        arrive(k)
+    for s in range(LATE):
+        share(s, theirs).wait_recv()
+        w_late[s] = w[s]
 
     def drain(i, _):
         to_sibling(i).wait_send()
-        for h in range(2):
-            share(i, h, mine).wait_send()
+        share(i, mine).wait_send()
         return 0
 
     lax.fori_loop(0, zs, drain, 0)
@@ -284,22 +273,28 @@
     lax.fori_loop(0, zs - 1, drain_ring, 0)
     for j in range(1, outs):
         to_peer(j).wait_send()
-    for h in range(2):
-        for t in range(4):
-            go_long(t, h).wait_send()
-        for t in range(3):
-            go_short(t, h).wait_send()
-    out_acc.wait()
-    out_pt.wait()
-    out_w.wait()
-
-
-def finish(acc, pt, w, re, im):
-    n = re.shape[1]
-    value = acc[...] + jnp.dot(pt[...], twice(w[...], n), preferred_element_type=F32)
+    for k in range(len(TREE)):
+        pass_on(k).wait_send()
+
+
+def finish(acc, pt, w, re_hbm, im_hbm, re, im, sem):
+    n, depth = re.shape[1], re.shape[0]
+    block = depth // PIECES
     norm = 1.0 / float(P_SIZE) ** 0.5
-    re[...] = value[:, :n] * norm
-    im[...] = value[:, n:] * norm
+    copies = []
+    for b in range(PIECES):
+        rows = slice(b * block, (b + 1) * block)
+        value = acc[rows, :]
+        for s in range(LATE):
+            value = value + jnp.dot(pt[s, rows, :], twice(w[s], n), preferred_element_type=F32)
+        re[rows, :] = value[:, :n] * norm
+        im[rows, :] = value[:, n:] * norm
+        for i, (here, there) in enumerate(((re, re_hbm), (im, im_hbm))):
+            there = there.at[pl.ds(b * block, block)]
+            copies.append(pltpu.make_async_copy(here.at[pl.ds(b * block, block)], there, sem.at[b, i]))
+            copies[-1].start()
+    for copy in copies:
+        copy.wait()
 
 
 def body(zs, outs, phases, transfer_re, transfer_im, measured):
@@ -309,21 +304,24 @@
     half = chunk // 2
     DMA = pltpu.SemaphoreType.DMA
     anywhere = pl.BlockSpec(memory_space=pl.ANY)
+    near = pl.BlockSpec(memory_space=pltpu.VMEM)
+    operands = [
+        pltpu.with_memory_space_constraint(v, pltpu.HBM)
+        for v in (phases, transfer_re, transfer_im, measured)
+    ]
     acc, pt, w = pl.pallas_call(
         functools.partial(front, zs, outs),
         out_shape=(
-            jax.ShapeDtypeStruct((depth, 2 * n), F32),
-            jax.ShapeDtypeStruct((depth, 2 * chunk), BF16),
-            jax.ShapeDtypeStruct((chunk, 2 * n), BF16),
+            pltpu.VMEM((depth, 2 * n), F32),
+            pltpu.VMEM((zs, depth, 2 * chunk), BF16),
+            pltpu.VMEM((LATE, chunk, 2 * n), BF16),
         ),
-        in_specs=[anywhere] * 4,
-        out_specs=(anywhere,) * 3,
+        in_specs=[pl.BlockSpec(memory_space=pltpu.HBM)] * 4,
+        out_specs=(near,) * 3,
         scratch_shapes=[
             pltpu.VMEM((zs, chunk, depth), BF16),
             pltpu.VMEM((2, depth, 2 * n), BF16),
             pltpu.VMEM((half, n), F32),
-            pltpu.VMEM((zs, depth, 2 * chunk), BF16),
-            pltpu.VMEM((depth, 2 * n), F32),
             pltpu.VMEM((zs, half, 2 * n), F32),
             pltpu.VMEM((zs, half, 2 * n), F32),
             pltpu.VMEM((zs, half, 2 * n), F32),
@@ -333,29 +331,25 @@
             pltpu.VMEM((outs, 8, half), F32),
             pltpu.VMEM((8, half), F32),
             pltpu.VMEM((zs, chunk, 2 * n), BF16),
-            DMA((zs,)), DMA((4,)), DMA((3,)),
+            DMA((zs,)), DMA((4,)),
             DMA((zs,)), DMA((zs,)),
             DMA((zs - 1, 2)), DMA((zs - 1, 2)),
             DMA((outs,)), DMA((outs,)),
-            DMA((4, 2)), DMA((4, 2)), DMA((3, 2)), DMA((3, 2)),
-            DMA((zs, 2)), DMA((zs, 2)),
+            DMA((len(TREE),)), DMA((len(TREE),)),
+            DMA((zs,)), DMA((zs,)),
         ],
         compiler_params=pltpu.CompilerParams(
-            collective_id=0, has_side_effects=True, vmem_limit_bytes=50 * 1024 * 1024
+            collective_id=0, has_side_effects=True, vmem_limit_bytes=24 * 1024 * 1024
         ),
-    )(phases, transfer_re, transfer_im, measured)
-    block = min(512, depth)
+    )(*operands)
     return pl.pallas_call(
         finish,
-        grid=(depth // block,),
         out_shape=(jax.ShapeDtypeStruct((depth, n), F32),) * 2,
-        in_specs=[
-            pl.BlockSpec((block, 2 * n), lambda b: (b, 0)),
-            pl.BlockSpec((block, 2 * chunk), lambda b: (b, 0)),
-            pl.BlockSpec((chunk, 2 * n), lambda b: (0, 0)),
-        ],
-        out_specs=(pl.BlockSpec((block, n), lambda b: (b, 0)),) * 2,
-    )(acc, pt, w)
+        in_specs=[near] * 3,
+        out_specs=(anywhere,) * 2,
+        scratch_shapes=[pltpu.VMEM((depth, n), F32)] * 2 + [DMA((PIECES, 2))],
+        compiler_params=pltpu.CompilerParams(vmem_limit_bytes=24 * 1024 * 1024),
+    )(*(pltpu.with_memory_space_constraint(v, pltpu.VMEM) for v in (acc, pt, w)))
 
 
 def solution(mesh):

time: 61.5 us -> 50.9 us (0.83); the launches traced: 60.8 us -> 50.8 us
  Pallas kernels: 56.1 us -> 50.2 us
  local copies, waits for them, and re-layouts: 4.06 us -> 0 us
    pallas_call x2, Pallas kernels: 56.1 us -> 50.2 us  [the longest x1 47.4 us: body(): pl.pallas_call(functools.partial(front, zs, outs), out_shape=(pltpu.VMEM(...]
    unnamed x8 -> x0, local copies, waits for them, and re-layouts: 4.06 us -> none
where the time goes in v2:
time: 50.9 us; the launch traced here: 50.8 us
  Pallas kernels  50.2 us (99%)
  between operations  0.64 us (1%)
    pallas_call x1, Pallas kernels, body(): pl.pallas_call(functools.partial(front, zs, outs), out_shape=(pltpu.VMEM(...  47.4 us
    pallas_call x1, Pallas kernels, body(): pl.pallas_call(finish, out_shape=(jax.ShapeDtypeStruct((depth, n), F32),)...  2.84 us

profile of v2, /device:TPU:1, one launch (start us, length us, event | category | flops | bytes accessed | tf_op | source)
XLA Modules:
  0.0 50.8 jit_solution(16282032991607034393)
XLA Ops:
  0.6 47.4 %shard_map.59 = (f32[2048,512]{1,0:T(8,128)S(1)}, bf16[8,2048,256]{2,1,0:T(8,128)(2,1)S(1)}, bf16[3,128,512]{2,1,0:T(8,128)(2,1)S(1)}) custom-call(bf16[1024,2048]{1,0:T(8,128)(2,1)} %ph_hbm.1, bf16[2048,256]{1,0:T(8,128)(2,1)} %tr_hbm.1, bf16[2048,256]{1,0:T(8,128)(2,1)} %ti_hbm.1, f32[1024,256]{1,0:T(8,128)} %me_hbm.1), custom_call_target="tpu_custom_call" | custom-call | tf_op jit(solution)/shard_map/pallas_call | solution.py:312
  48.0 2.8 %shard_map.60 = (f32[2048,256]{1,0:T(8,128)}, f32[2048,256]{1,0:T(8,128)}) custom-call(f32[2048,512]{1,0:T(8,128)S(1)} %get-tuple-element.5.acc, bf16[8,2048,256]{2,1,0:T(8,128)(2,1)S(1)} %get-tuple-element.6.pt, bf16[3,128,512]{2,1,0:T(8,128)(2,1)S(1)} %get-tuple-element.7.w), custom_call_target="tpu_custom_call" | custom-call | tf_op jit(solution)/shard_map/pallas_call | solution.py:345

commit v3 on v2

v3 whole, which is shorter than its diff:
```python
import functools

import jax
import jax.numpy as jnp
from jax import lax
from jax.experimental import pallas as pl
from jax.experimental.pallas import tpu as pltpu
from jax.sharding import PartitionSpec as P

P_SIZE = 1024
MESH = pl.DeviceIdType.MESH
TREE = ((0, 2), (0, -2), (0, 1), (0, -1), (2, 4), (2, 3), (-2, -3))
LATE = 3
PIECES = 8
JOIN = (5, 6)
PARTS = 2
SUBS = 2
F32 = jnp.float32
BF16 = jnp.bfloat16
SIN = (7.07104388e-01, -2.94595328e-02, 3.67091170e-04, -2.02891555e-06)
COS = (1.41420408e00, -1.76745738e-01, 3.66703335e-03, -2.80900148e-05)


def cos_sin(x):
    u = x * x
    s = x * (SIN[0] + u * (SIN[1] + u * (SIN[2] + u * SIN[3])))
    c = COS[0] + u * (COS[1] + u * (COS[2] + u * COS[3]))
    return 1.0 - s * s, s * c


def twice(w, n):
    return jnp.concatenate([w, jnp.concatenate([w[:, n:], -w[:, :n]], axis=1)], axis=0)


def front(
    zs, outs, ph_hbm, tr_hbm, ti_hbm, me_hbm, acc, pt, w_late,
    ph, rhs, meas, part, give, sib, ring, send, ring16, send16, field, pw, pws, w,
    in_sem, t_sem, sib_s, sib_r, far_s, far_r, ring_s, ring_r, pw_s, pw_r, ag_s, ag_r, agb_s, agb_r,
):
    chunk, half, n = ph.shape[1], ph.shape[1] // 2, meas.shape[1]
    depth, slab = ph.shape[2], min(256, ph.shape[2])
    sub = half // SUBS
    me = lax.axis_index("inp")
    peer = lax.axis_index("out")
    z, core = me // 2, me % 2
    step = 1 - 2 * core

    def at(d):
        return lax.rem(z + step * d + zs, zs) * 2 + core

    other = z * 2 + 1 - core
    up, down = lax.rem(z + 1, zs) * 2 + core, lax.rem(z + zs - 1, zs) * 2 + core
    mine = pl.multiple_of(core * half, half)
    theirs = pl.multiple_of((1 - core) * half, half)

    def chunk_of(i):
        off = jnp.where(i % 2 == 1, 4 - (i + 1) // 2, i // 2 - 4)
        return lax.rem(z + off + zs, zs)

    def load_phase(i):
        rows = pl.ds(pl.multiple_of(chunk_of(i) * chunk, chunk), chunk)
        return pltpu.make_async_copy(ph_hbm.at[rows], ph.at[i], in_sem.at[i])

    loads = []
    for j in range(PARTS):
        rows = pl.ds(j * (depth // PARTS), depth // PARTS)
        loads.append(
            [
                pltpu.make_async_copy(
                    source.at[rows], rhs.at[0, rows, pl.ds(k * n, n)], t_sem.at[j, k]
                )
                for k, source in enumerate((tr_hbm, ti_hbm))
            ]
        )
    load_phase(0).start()
    for pair in loads:
        for copy in pair:
            copy.start()
    for i in range(1, zs):
        load_phase(i).start()
    own_rows = pl.ds(pl.multiple_of(z * chunk + core * half, half), half)
    load_meas = pltpu.make_async_copy(me_hbm.at[own_rows], meas, t_sem.at[PARTS, 0])
    load_meas.start()

    barrier = pltpu.get_barrier_semaphore()
    for target in (other, up, down, at(2), at(-2)):
        pl.semaphore_signal(barrier, inc=1, device_id={"inp": target}, device_id_type=MESH)
    for j in range(1, outs):
        pl.semaphore_signal(
            barrier, inc=1, device_id={"out": lax.rem(peer + j, outs)}, device_id_type=MESH
        )

    def to_sibling(i):
        return pltpu.make_async_remote_copy(
            src_ref=give.at[i], dst_ref=sib.at[i], send_sem=sib_s.at[i], recv_sem=sib_r.at[i],
            device_id={"inp": other}, device_id_type=MESH,
        )

    def hop16(i):
        target = jnp.where(i == 0, at(2), jnp.where(i == 1, up, down))
        return pltpu.make_async_remote_copy(
            src_ref=send16.at[i], dst_ref=ring16.at[i],
            send_sem=far_s.at[i], recv_sem=far_r.at[i],
            device_id={"inp": target}, device_id_type=MESH,
        )

    def hop32(i, h):
        rows = pl.ds(h * sub, sub)
        return pltpu.make_async_remote_copy(
            src_ref=send.at[i - 3, rows], dst_ref=ring.at[i - 3, rows],
            send_sem=ring_s.at[i - 3, h], recv_sem=ring_r.at[i - 3, h],
            device_id={"inp": up if i % 2 == 1 else down}, device_id_type=MESH,
        )

    def forward(i, first=False):
        load_phase(i).wait()
        total = None
        for j in range(depth // slab):
            cols = slice(j * slab, (j + 1) * slab)
            if first and j % (depth // slab // PARTS) == 0:
                part_no = j // (depth // slab // PARTS)
                for copy in loads[part_no]:
                    copy.wait()
                rows = slice(part_no * (depth // PARTS), (part_no + 1) * (depth // PARTS))
                rhs[1, rows, 0:n] = -rhs[0, rows, n:]
                rhs[1, rows, n:] = rhs[0, rows, 0:n]
            re, im = cos_sin(ph[i, :, cols].astype(F32))
            re, im = re.astype(BF16), im.astype(BF16)
            pt[i, cols, 0:chunk] = re.T
            pt[i, cols, chunk:] = im.T
            left = jnp.concatenate([re, im], axis=1)
            right = jnp.concatenate([rhs[0, cols, :], rhs[1, cols, :]], axis=0)
            term = jnp.dot(left, right, preferred_element_type=F32)
            total = term if total is None else total + term
        field[...] = total
        part[i] = field[pl.ds(mine, half), :]
        give[i] = field[pl.ds(theirs, half), :]

    def pass_single(i):
        to_sibling(i).wait_recv()
        send16[i] = (part[i] + sib[i]).astype(BF16)
        hop16(i).start()

    def pass_joint(i):
        to_sibling(i).wait_recv()
        hop16(i - 2).wait_recv()

        @pl.when(core == i - 3)
        def _():
            hop16(0).wait_recv()

        for h in range(SUBS):
            rows = slice(h * sub, (h + 1) * sub)
            value = part[i, rows, :] + sib[i, rows, :] + ring16[i - 2, rows, :].astype(F32)

            @pl.when(core == i - 3)
            def _():
                send[i - 3, rows, :] = value + ring16[0, rows, :].astype(F32)

            @pl.when(core != i - 3)
            def _():
                send[i - 3, rows, :] = value

            hop32(i, h).start()

    def pass_last(i, h):
        rows = slice(h * sub, (h + 1) * sub)
        value = part[i, rows, :] + sib[i, rows, :]
        hop32(i - 2, h).wait_recv()
        send[i - 3, rows, :] = value + ring[i - 5, rows, :]
        hop32(i, h).start()

    forward(0, True)
    pl.semaphore_wait(barrier, 5 + outs - 1)
    to_sibling(0).start()

    def body(i, _):
        forward(i)
        to_sibling(i).start()

        @pl.when(i < 4)
        def _():
            pass_single(i - 1)

        @pl.when(i == JOIN[0])
        def _():
            pass_joint(3)

        @pl.when(i == JOIN[1])
        def _():
            pass_joint(4)

        return 0

    lax.fori_loop(1, zs, body, 0)
    for i in (5, 6):
        to_sibling(i).wait_recv()
    for i in (5, 6):
        for h in range(SUBS):
            pass_last(i, h)

    def lane_sum(v):
        folded = v[:, 0:128]
        for k in range(1, n // 128):
            folded = folded + v[:, k * 128 : (k + 1) * 128]
        return jnp.sum(folded.T, axis=0, keepdims=True)

    load_meas.wait()
    light = meas[...]
    light_sum = lane_sum(light)
    to_sibling(zs - 1).wait_recv()
    total = part[zs - 1] + sib[zs - 1]
    for i in (5, 6):
        for h in range(SUBS):
            hop32(i, h).wait_recv()
        total = total + ring[i - 3]
    f_re, f_im = total[:, :n], total[:, n:]
    power = f_re * f_re + f_im * f_im
    pws[:, 0:half] = lane_sum(power)
    pws[:, half:] = light_sum

    def to_peer(j):
        return pltpu.make_async_remote_copy(
            src_ref=pws, dst_ref=pw.at[j], send_sem=pw_s.at[j], recv_sem=pw_r.at[j],
            device_id={"out": lax.rem(peer + j, outs)}, device_id_type=MESH,
        )

    for j in range(1, outs):
        to_peer(j).start()
    sums = pws[...]
    for j in range(1, outs):
        to_peer(j).wait_recv()
        sums = sums + pw[j]
    scale = sums[:, half:] / (sums[:, 0:half] + 1e-05)
    scale = jnp.broadcast_to(scale, (128, half)).T
    scale = jnp.concatenate([scale] * (n // 128), axis=1)
    factor = scale * (scale * power - light)
    own = pl.ds(mine, half)
    w[zs - 1, own, 0:n] = (factor * f_re).astype(BF16)
    w[zs - 1, own, n:] = (factor * f_im).astype(BF16)

    def slot_of(d):
        if d == 0:
            return zs - 1
        if d == 4:
            return 0
        return 8 - 2 * d - core if d > 0 else 7 + 2 * d + core

    def pass_on(k, h):
        d, there = TREE[k]
        rows = pl.ds(pl.multiple_of(mine + h * sub, sub), sub)
        return pltpu.make_async_remote_copy(
            src_ref=w.at[slot_of(d), rows], dst_ref=w.at[slot_of(there), rows],
            send_sem=ag_s.at[k, h], recv_sem=ag_r.at[k, h],
            device_id={"inp": at(there - d)}, device_id_type=MESH,
        )

    def share(slot, h, rows0):
        rows = pl.ds(pl.multiple_of(rows0 + h * sub, sub), sub)
        return pltpu.make_async_remote_copy(
            src_ref=w.at[slot, rows], dst_ref=w.at[slot, rows],
            send_sem=agb_s.at[slot, h], recv_sem=agb_r.at[slot, h],
            device_id={"inp": other}, device_id_type=MESH,
        )

    def arrive(group):
        for h in range(SUBS):
            for k in group:
                pass_on(k, h).wait_recv()
                for later in range(len(TREE)):
                    if TREE[later][0] == TREE[k][1]:
                        pass_on(later, h).start()
                share(slot_of(TREE[k][1]), h, mine).start()

    block = min(512, depth)

    def backward(slots, first):
        for s in slots:
            for h in range(SUBS):
                share(s, h, theirs).wait_recv()

        def rows_of(b, _):
            rows = pl.ds(pl.multiple_of(b * block, block), block)
            value = None
            for s in slots:
                term = jnp.dot(pt[s, rows, :], twice(w[s], n), preferred_element_type=F32)
                value = term if value is None else value + term
            if not first:
                value = value + acc[rows, :]
            acc[rows, :] = value
            return 0

        lax.fori_loop(0, depth // block, rows_of, 0)

    for group in ((0, 1), (2, 3)):
        for h in range(SUBS):
            for k in group:
                pass_on(k, h).start()
    for h in range(SUBS):
        share(zs - 1, h, mine).start()
    backward((zs - 1,), True)
    arrive((0, 1))
    arrive((2, 3))
    backward((3, 4, 5, 6), False)

    def drain(i, _):
        to_sibling(i).wait_send()
        return 0

    lax.fori_loop(0, zs, drain, 0)
    for i in range(3):
        hop16(i).wait_send()
    for i in range(3, 7):
        for h in range(SUBS):
            hop32(i, h).wait_send()
    for j in range(1, outs):
        to_peer(j).wait_send()
    for k in range(4):
        for h in range(SUBS):
            pass_on(k, h).wait_send()

    arrive((4, 5, 6))
    for s in range(LATE):
        for h in range(SUBS):
            share(s, h, theirs).wait_recv()
        w_late[s] = w[s]
    for k in range(4, len(TREE)):
        for h in range(SUBS):
            pass_on(k, h).wait_send()
    for s in range(zs):
        for h in range(SUBS):
            share(s, h, mine).wait_send()


def finish(acc, pt, w, re_hbm, im_hbm, re, im, sem):
    n, depth = re.shape[1], re.shape[0]
    block = depth // PIECES
    norm = 1.0 / float(P_SIZE) ** 0.5
    copies = []
    for b in range(PIECES):
        rows = slice(b * block, (b + 1) * block)
        value = acc[rows, :]
        for s in range(LATE):
            value = value + jnp.dot(pt[s, rows, :], twice(w[s], n), preferred_element_type=F32)
        re[rows, :] = value[:, :n] * norm
        im[rows, :] = value[:, n:] * norm
        for i, (here, there) in enumerate(((re, re_hbm), (im, im_hbm))):
            there = there.at[pl.ds(b * block, block)]
            copies.append(pltpu.make_async_copy(here.at[pl.ds(b * block, block)], there, sem.at[b, i]))
            copies[-1].start()
    for copy in copies:
        copy.wait()


def body(zs, outs, phases, transfer_re, transfer_im, measured):
    probes, depth = phases.shape
    n = transfer_re.shape[1]
    chunk = probes // zs
    half = chunk // 2
    DMA = pltpu.SemaphoreType.DMA
    anywhere = pl.BlockSpec(memory_space=pl.ANY)
    near = pl.BlockSpec(memory_space=pltpu.VMEM)
    operands = [
        pltpu.with_memory_space_constraint(v, pltpu.HBM)
        for v in (phases, transfer_re, transfer_im, measured)
    ]
    acc, pt, w = pl.pallas_call(
        functools.partial(front, zs, outs),
        out_shape=(
            pltpu.VMEM((depth, 2 * n), F32),
            pltpu.VMEM((zs, depth, 2 * chunk), BF16),
            pltpu.VMEM((LATE, chunk, 2 * n), BF16),
        ),
        in_specs=[pl.BlockSpec(memory_space=pltpu.HBM)] * 4,
        out_specs=(near,) * 3,
        scratch_shapes=[
            pltpu.VMEM((zs, chunk, depth), BF16),
            pltpu.VMEM((2, depth, 2 * n), BF16),
            pltpu.VMEM((half, n), F32),
            pltpu.VMEM((zs, half, 2 * n), F32),
            pltpu.VMEM((zs, half, 2 * n), F32),
            pltpu.VMEM((zs, half, 2 * n), F32),
            pltpu.VMEM((4, half, 2 * n), F32),
            pltpu.VMEM((4, half, 2 * n), F32),
            pltpu.VMEM((3, half, 2 * n), BF16),
            pltpu.VMEM((3, half, 2 * n), BF16),
            pltpu.VMEM((chunk, 2 * n), F32),
            pltpu.VMEM((outs, 1, 2 * half), F32),
            pltpu.VMEM((1, 2 * half), F32),
            pltpu.VMEM((zs, chunk, 2 * n), BF16),
            DMA((zs,)), DMA((PARTS + 1, 2)),
            DMA((zs,)), DMA((zs,)),
            DMA((3,)), DMA((3,)), DMA((4, SUBS)), DMA((4, SUBS)),
            DMA((outs,)), DMA((outs,)),
            DMA((len(TREE), SUBS)), DMA((len(TREE), SUBS)),
            DMA((zs, SUBS)), DMA((zs, SUBS)),
        ],
        compiler_params=pltpu.CompilerParams(
            collective_id=0, has_side_effects=True, vmem_limit_bytes=24 * 1024 * 1024
        ),
    )(*operands)
    return pl.pallas_call(
        finish,
        out_shape=(jax.ShapeDtypeStruct((depth, n), F32),) * 2,
        in_specs=[near] * 3,
        out_specs=(anywhere,) * 2,
        scratch_shapes=[pltpu.VMEM((depth, n), F32)] * 2 + [DMA((PIECES, 2))],
        compiler_params=pltpu.CompilerParams(vmem_limit_bytes=24 * 1024 * 1024),
    )(*(pltpu.with_memory_space_constraint(v, pltpu.VMEM) for v in (acc, pt, w)))


def solution(mesh):
    in_specs = (P(None, "inp"), P("inp", "out"), P("inp", "out"), P(None, "out"))
    out_specs = (P("inp", "out"), P("inp", "out"))
    fn = functools.partial(body, mesh.shape["inp"] // 2, mesh.shape["out"])
    return jax.shard_map(fn, mesh=mesh, in_specs=in_specs, out_specs=out_specs, check_vma=False)
```

time: 50.9 us -> 47.8 us (0.939)
  Pallas kernels: 50.2 us -> 47 us
    pallas_call x1, Pallas kernels: 47.4 us -> 44.3 us  [body(): pl.pallas_call(functools.partial(front, zs, outs), out_shape=(pltpu.VMEM(...]
where the time goes in v3:
time: 47.8 us; the launch traced here: 47.7 us
  Pallas kernels  47 us (98%)
  between operations  0.64 us (1%)
    pallas_call x1, Pallas kernels, body(): pl.pallas_call(functools.partial(front, zs, outs), out_shape=(pltpu.VMEM(...  44.3 us
    pallas_call x1, Pallas kernels, body(): pl.pallas_call(finish, out_shape=(jax.ShapeDtypeStruct((depth, n), F32),)...  2.73 us

profile of v3, /device:TPU:1, one launch (start us, length us, event | category | flops | bytes accessed | tf_op | source)
XLA Modules:
  0.0 47.7 jit_solution(12115269122689823778)
XLA Ops:
  0.6 44.3 %shard_map.59 = (f32[2048,512]{1,0:T(8,128)S(1)}, bf16[8,2048,256]{2,1,0:T(8,128)(2,1)S(1)}, bf16[3,128,512]{2,1,0:T(8,128)(2,1)S(1)}) custom-call(bf16[1024,2048]{1,0:T(8,128)(2,1)} %ph_hbm.1, bf16[2048,256]{1,0:T(8,128)(2,1)} %tr_hbm.1, bf16[2048,256]{1,0:T(8,128)(2,1)} %ti_hbm.1, f32[1024,256]{1,0:T(8,128)} %me_hbm.1), custom_call_target="tpu_custom_call" | custom-call | tf_op jit(solution)/shard_map/pallas_call | solution.py:367
  45.0 2.7 %shard_map.60 = (f32[2048,256]{1,0:T(8,128)}, f32[2048,256]{1,0:T(8,128)}) custom-call(f32[2048,512]{1,0:T(8,128)S(1)} %get-tuple-element.5.acc, bf16[8,2048,256]{2,1,0:T(8,128)(2,1)S(1)} %get-tuple-element.6.pt, bf16[3,128,512]{2,1,0:T(8,128)(2,1)S(1)} %get-tuple-element.7.w), custom_call_target="tpu_custom_call" | custom-call | tf_op jit(solution)/shard_map/pallas_call | solution.py:402

commit v4 on v3

--- a/solution.py
+++ b/solution.py
@@ -13,7 +13,8 @@
 LATE = 3
 PIECES = 8
 JOIN = (5, 6)
-PARTS = 2
+PARTS = 4
+HOPS = 4
 SUBS = 2
 F32 = jnp.float32
 BF16 = jnp.bfloat16
@@ -105,7 +106,7 @@
         )
 
     def hop32(i, h):
-        rows = pl.ds(h * sub, sub)
+        rows = pl.ds(h * (half // HOPS), half // HOPS)
         return pltpu.make_async_remote_copy(
             src_ref=send.at[i - 3, rows], dst_ref=ring.at[i - 3, rows],
             send_sem=ring_s.at[i - 3, h], recv_sem=ring_r.at[i - 3, h],
@@ -149,8 +150,8 @@
         def _():
             hop16(0).wait_recv()
 
-        for h in range(SUBS):
-            rows = slice(h * sub, (h + 1) * sub)
+        for h in range(HOPS):
+            rows = slice(h * (half // HOPS), (h + 1) * (half // HOPS))
             value = part[i, rows, :] + sib[i, rows, :] + ring16[i - 2, rows, :].astype(F32)
 
             @pl.when(core == i - 3)
@@ -164,7 +165,7 @@
             hop32(i, h).start()
 
     def pass_last(i, h):
-        rows = slice(h * sub, (h + 1) * sub)
+        rows = slice(h * (half // HOPS), (h + 1) * (half // HOPS))
         value = part[i, rows, :] + sib[i, rows, :]
         hop32(i - 2, h).wait_recv()
         send[i - 3, rows, :] = value + ring[i - 5, rows, :]
@@ -195,8 +196,8 @@
     lax.fori_loop(1, zs, body, 0)
     for i in (5, 6):
         to_sibling(i).wait_recv()
-    for i in (5, 6):
-        for h in range(SUBS):
+    for h in range(HOPS):
+        for i in (5, 6):
             pass_last(i, h)
 
     def lane_sum(v):
@@ -211,7 +212,7 @@
     to_sibling(zs - 1).wait_recv()
     total = part[zs - 1] + sib[zs - 1]
     for i in (5, 6):
-        for h in range(SUBS):
+        for h in range(HOPS):
             hop32(i, h).wait_recv()
         total = total + ring[i - 3]
     f_re, f_im = total[:, :n], total[:, n:]
@@ -272,25 +273,20 @@
                         pass_on(later, h).start()
                 share(slot_of(TREE[k][1]), h, mine).start()
 
-    block = min(512, depth)
+    block = min(256, depth)
 
     def backward(slots, first):
         for s in slots:
             for h in range(SUBS):
                 share(s, h, theirs).wait_recv()
 
-        def rows_of(b, _):
-            rows = pl.ds(pl.multiple_of(b * block, block), block)
-            value = None
+        for b in range(depth // block):
+            rows = slice(b * block, (b + 1) * block)
+            value = None if first else acc[rows, :]
             for s in slots:
                 term = jnp.dot(pt[s, rows, :], twice(w[s], n), preferred_element_type=F32)
                 value = term if value is None else value + term
-            if not first:
-                value = value + acc[rows, :]
             acc[rows, :] = value
-            return 0
-
-        lax.fori_loop(0, depth // block, rows_of, 0)
 
     for group in ((0, 1), (2, 3)):
         for h in range(SUBS):
@@ -311,7 +307,7 @@
     for i in range(3):
         hop16(i).wait_send()
     for i in range(3, 7):
-        for h in range(SUBS):
+        for h in range(HOPS):
             hop32(i, h).wait_send()
     for j in range(1, outs):
         to_peer(j).wait_send()
@@ -390,7 +386,7 @@
             pltpu.VMEM((zs, chunk, 2 * n), BF16),
             DMA((zs,)), DMA((PARTS + 1, 2)),
             DMA((zs,)), DMA((zs,)),
-            DMA((3,)), DMA((3,)), DMA((4, SUBS)), DMA((4, SUBS)),
+            DMA((3,)), DMA((3,)), DMA((4, HOPS)), DMA((4, HOPS)),
             DMA((outs,)), DMA((outs,)),
             DMA((len(TREE), SUBS)), DMA((len(TREE), SUBS)),
             DMA((zs, SUBS)), DMA((zs, SUBS)),

time: 47.8 us -> 46.9 us (0.981)
  Pallas kernels: 47 us -> 46.1 us
    pallas_call x1, Pallas kernels: 44.3 us -> 43.4 us  [body(): pl.pallas_call(functools.partial(front, zs, outs), out_shape=(pltpu.VMEM(...]
where the time goes in v4:
time: 46.9 us; the launch traced here: 46.8 us
  Pallas kernels  46.1 us (98%)
  between operations  0.64 us (1%)
    pallas_call x1, Pallas kernels, body(): pl.pallas_call(functools.partial(front, zs, outs), out_shape=(pltpu.VMEM(...  43.4 us
    pallas_call x1, Pallas kernels, body(): pl.pallas_call(finish, out_shape=(jax.ShapeDtypeStruct((depth, n), F32),)...  2.74 us

profile of v4, /device:TPU:1, one launch (start us, length us, event | category | flops | bytes accessed | tf_op | source)
XLA Modules:
  0.0 46.8 jit_solution(5434901075072532916)
XLA Ops:
  0.6 43.4 %shard_map.59 = (f32[2048,512]{1,0:T(8,128)S(1)}, bf16[8,2048,256]{2,1,0:T(8,128)(2,1)S(1)}, bf16[3,128,512]{2,1,0:T(8,128)(2,1)S(1)}) custom-call(bf16[1024,2048]{1,0:T(8,128)(2,1)} %ph_hbm.1, bf16[2048,256]{1,0:T(8,128)(2,1)} %tr_hbm.1, bf16[2048,256]{1,0:T(8,128)(2,1)} %ti_hbm.1, f32[1024,256]{1,0:T(8,128)} %me_hbm.1), custom_call_target="tpu_custom_call" | custom-call | tf_op jit(solution)/shard_map/pallas_call | solution.py:363
  44.0 2.7 %shard_map.60 = (f32[2048,256]{1,0:T(8,128)}, f32[2048,256]{1,0:T(8,128)}) custom-call(f32[2048,512]{1,0:T(8,128)S(1)} %get-tuple-element.5.acc, bf16[8,2048,256]{2,1,0:T(8,128)(2,1)S(1)} %get-tuple-element.6.pt, bf16[3,128,512]{2,1,0:T(8,128)(2,1)S(1)} %get-tuple-element.7.w), custom_call_target="tpu_custom_call" | custom-call | tf_op jit(solution)/shard_map/pallas_call | solution.py:398
